TPU v7x, 32 devices: a whole 2x2x4 slice. The times are simulated.
32 devices in a mesh: date: 2 (over y), trade: 8 (over z, x), path: 2 (over core).
Axes of the slice: x: 2, y: 2, z: 4, core: 2. Of those that a mesh axis runs over, the one named last changes fastest.
Arguments:
- basis_values: bfloat16 [2048, 512], P(('date', 'path')), parts along dimension 0, may hold values from -6 to 6
- coefficients: bfloat16 [2560, 512], P(('date', 'trade')), parts along dimension 0, may hold values from -0.25 to 0.25
- trade_cpty: int32 [1280], P('trade'), may hold values from 0 to 127, as said below
- trade_bucket: int32 [1280], P('trade'), may hold values from 0 to 127
- risk_weights: float32 [128], replicated, may hold values from 0.5 to 2
- correlation: float32 [128, 128], replicated, may hold values from 0 to 1, as said below
- funding_spread: float32 [128], P('trade'), may hold values from 0.5 to 2
Outputs:
- margin: float32 [128, 2048], P('trade', ('date', 'path')), parts along dimension 1
- basis_adjoint: bfloat16 [2048, 512], P(('date', 'path')), parts along dimension 0
There are 2 independent parts, one for each index of `date`. A program takes and returns all parts, laid end to end along the dimension named above; an argument that names none is the same for every part. Nothing has to cross between parts.
Inputs may be any that keep to these rules, and one draw needn't show every extreme that they name: `trade_cpty`: counterparty c belongs to owner block c // 16. Among the trades of one device, at most 40 belong to counterparties of one owner block; in every draw one owner block receives exactly 40 from every device. Counterparties differ in size. `correlation`: symmetric positive definite with unit diagonal; smallest eigenvalue at least 0.01; entries positive.
All inputs are finite; a program needn't handle non-finite values.
Results may differ from a plain program's by a relative error of at most 0.0034.
Values may be sent and summed in bfloat16 or wider, within the bound.
A program may use at most 64 MiB of HBM per device.

v0:
```python
import functools
import jax
import jax.numpy as jnp
from jax import lax
from jax.experimental import pallas as pl
from jax.experimental.pallas import tpu as pltpu
from jax.sharding import PartitionSpec as P

MESH = pl.DeviceIdType.MESH
TERMS = 2
PIECES = 2
ADJ_PIECES = 4
DEEP = 4


def split_terms(value, count):
    parts = []
    for _ in range(count):
        head = value.astype(jnp.bfloat16)
        parts.append(head)
        value = value - head.astype(jnp.float32)
    return parts


def dot_nt(a, b):
    return lax.dot_general(a, b, (((1,), (1,)), ((), ())), preferred_element_type=jnp.float32)


def dot_nn(a, b):
    return jnp.dot(a, b, preferred_element_type=jnp.float32)


def margin_kernel(
    owners, basis_in, coef_in, cpty_in, bucket_in, rw_in, corr_in, spread_in,
    adj_out, margin_out,
    held, adj_ref, margin_ref, rows_buf, cpty_buf, bucket_buf, rw_buf, corr_buf, spread_buf,
    msg, msgs, gram, cols_buf, bucket_hot, cpty_hot, cpty_cols, bar_buf, msend, mrecv,
    local, zu, zd, zr, xs, xr, cs, cr, gs, gr, ms, mr, az_u, az_d, az_r, ax_s, ax_r, outs,
):
    t = lax.axis_index("trade")
    k = lax.axis_index("path")
    z = t // 2
    x = t % 2
    per_device, width = coef_in.shape
    half = per_device // 2
    span = width // PIECES
    adj_span = width // ADJ_PIECES
    buckets = corr_in.shape[0]
    trades = owners * per_device
    path_share = rows_buf.shape[0]
    cpty_dev = mrecv.shape[1]
    cptys = owners * cpty_dev
    code_lanes = -(-per_device // 128) * 128

    def slot(zz, xx, rz, rx):
        return (xx + rx) % 2 * 4 + (zz // 2 + rz // 2) % 2 * 2 + zz % 2

    def send(src, dst, send_sem, recv_sem, to_trade, to_path):
        return pltpu.make_async_remote_copy(
            src_ref=src, dst_ref=dst, send_sem=send_sem, recv_sem=recv_sem,
            device_id={"trade": to_trade, "path": to_path}, device_id_type=MESH,
        )

    own = slot(z, x, z, x)
    small = [
        pltpu.make_async_copy(cpty_in, cpty_buf, local.at[0]),
        pltpu.make_async_copy(bucket_in, bucket_buf, local.at[1]),
        pltpu.make_async_copy(spread_in, spread_buf, local.at[2]),
    ]
    shard = [
        pltpu.make_async_copy(
            coef_in.at[pl.ds(kk * half, half)], held.at[own * 2 + kk], local.at[3 + kk]
        )
        for kk in range(2)
    ]
    rest = [
        pltpu.make_async_copy(rw_in, rw_buf, local.at[5]),
        pltpu.make_async_copy(corr_in, corr_buf, local.at[6]),
        pltpu.make_async_copy(
            basis_in.at[pl.ds(pl.multiple_of(t * path_share, 16), path_share)], rows_buf, local.at[7]
        ),
    ]
    for copy in small + shard + rest:
        copy.start()

    barrier = pltpu.get_barrier_semaphore()
    for step in range(1, owners):
        pl.semaphore_signal(
            barrier, inc=1, device_id={"trade": (t + step) % owners, "path": k}, device_id_type=MESH
        )
    pl.semaphore_signal(barrier, inc=1, device_id={"trade": t, "path": 1 - k}, device_id_type=MESH)

    for copy in small:
        copy.wait()
    msg[...] = jnp.zeros_like(msg)
    msg[:, :per_device] = (cpty_buf[...] * buckets + bucket_buf[...]).astype(jnp.float32)
    msg[:, code_lanes:code_lanes + cpty_dev] = spread_buf[...]
    msgs[0] = msg[...]
    for copy in shard:
        copy.wait()
    pl.semaphore_wait(barrier, owners)

    def msg_copy(step):
        return send(msg, msgs.at[step], gs.at[step], gr.at[step], (t + step) % owners, k)

    def piece(where, p):
        return held.at[where * 2 + k, :, pl.ds(p * span, span)]

    def hop(zz, xx, p, sems, arrive, rz, rx):
        return send(
            piece(slot(zz, xx, z, x), p), piece(slot(zz, xx, rz, rx), p),
            sems.at[zz * PIECES + p], arrive.at[zz * PIECES + p], rz * 2 + rx, k,
        )

    def up(zz, p):
        return hop(zz, x, p, zu, zr, z + 1, x)

    def down(zz, p):
        return hop(zz, x, p, zd, zr, z - 1, x)

    def across(zz, p):
        return hop(zz, x, p, xs, xr, z, 1 - x)

    def over(where, p):
        ref = piece(where, p)
        sem = where * PIECES + p
        return send(ref, ref, cs.at[sem], cr.at[sem], t, 1 - k)

    def chain_arrived(zz, p):
        ref = piece(slot(zz, x, z, x), p)
        sem = zz * PIECES + p
        send(ref, ref, zu.at[sem], zr.at[sem], z * 2 + 1 - x, k).wait_recv()

    def across_arrived(zz, p):
        ref = piece(slot(zz, 1 - x, z, x), p)
        sem = zz * PIECES + p
        send(ref, ref, xs.at[sem], xr.at[sem], z * 2 + 1 - x, k).wait_recv()

    for p in range(PIECES):
        @pl.when(z < DEEP - 1)
        def _():
            up(z, p).start()

        @pl.when(z > 0)
        def _():
            down(z, p).start()

        across(z, p).start()
        if p == 0:
            for step in range(1, owners):
                msg_copy(step).start()

    def chain_arrival(j, p):
        @pl.when(z - j >= 0)
        def _():
            zz = z - j
            chain_arrived(zz, p)

            @pl.when(z < DEEP - 1)
            def _():
                up(zz, p).start()
            across(zz, p).start()
            over(slot(zz, x, z, x), p).start()

        @pl.when(z + j < DEEP)
        def _():
            zz = z + j
            chain_arrived(zz, p)

            @pl.when(z > 0)
            def _():
                down(zz, p).start()
            across(zz, p).start()
            over(slot(zz, x, z, x), p).start()

    def across_at(zz, p):
        across_arrived(zz, p)
        over(slot(zz, 1 - x, z, x), p).start()

    def across_arrival(j, p):
        if j == 0:
            across_at(z, p)
            return

        @pl.when(z - j >= 0)
        def _():
            across_at(z - j, p)

        @pl.when(z + j < DEEP)
        def _():
            across_at(z + j, p)

    for copy in rest:
        copy.wait()
    rw_rows = jnp.broadcast_to(rw_buf[...], (buckets, buckets))
    scaled = corr_buf[...] * rw_rows * rw_rows.T
    scaled_terms = jnp.concatenate(split_terms(scaled, TERMS), axis=1)

    chain_arrival(1, 0)
    chain_arrival(1, 1)
    for step in range(1, owners):
        msg_copy(step).wait_recv()

    def sender(i):
        zz = (i // 2 + z // 2) % 2 * 2 + i % 2
        return zz * 2 + (i // 4 + x) % 2

    codes = jnp.concatenate(
        [msgs[(t - sender(i)) % owners][:, :per_device] for i in range(owners)], axis=1
    ).astype(jnp.int32)
    spread = jnp.concatenate(
        [msgs[(t - o) % owners][:, code_lanes:code_lanes + cpty_dev] for o in range(owners)], axis=1
    )
    cpty_row = codes // buckets
    bucket_row = codes % buckets
    bucket_hot[...] = (
        lax.broadcasted_iota(jnp.int32, (buckets, trades), 0) == bucket_row
    ).astype(jnp.float32).astype(jnp.bfloat16)
    cpty_hot[...] = (
        lax.broadcasted_iota(jnp.int32, (cptys, trades), 0) == cpty_row
    ).astype(jnp.float32).astype(jnp.bfloat16)
    cols_buf[...] = jnp.broadcast_to(codes.astype(jnp.float32), (8, trades)).T.astype(jnp.int32)

    def build(first, last):
        @pl.loop(first, last)
        def _(i):
            rows = pl.ds(pl.multiple_of(i * per_device, 16), per_device)
            code_col = cols_buf[rows, :1]
            hot = (
                lax.broadcasted_iota(jnp.int32, (per_device, buckets), 1) == code_col % buckets
            ).astype(jnp.float32).astype(jnp.bfloat16)
            same = code_col // buckets == cpty_row
            cpty_cols[rows, :] = (
                lax.broadcasted_iota(jnp.int32, (per_device, cptys), 1) == code_col // buckets
            ).astype(jnp.float32).astype(jnp.bfloat16)
            picked = dot_nn(hot, scaled_terms).astype(jnp.bfloat16)
            stacked = jnp.concatenate(
                [picked[:, term * buckets:(term + 1) * buckets] for term in range(TERMS)], axis=0
            )
            blocks = dot_nn(stacked, bucket_hot[...])
            for term in range(TERMS):
                block = blocks[term * per_device:(term + 1) * per_device]
                gram[term, rows, :] = jnp.where(same, block, 0.0).astype(jnp.bfloat16)

    def deltas(first, last):
        for where in range(2 * first, 2 * last):
            for p in range(PIECES):
                if where < 2:
                    @pl.when(where != own)
                    def _():
                        over(where, p).wait_recv()
                else:
                    over(where, p).wait_recv()
        rows = slice(first * 2 * per_device, last * 2 * per_device)
        coef_rows = held[first * 4:last * 4].reshape((last - first) * 2 * per_device, width)
        delta = dot_nt(rows_buf[...], coef_rows).astype(jnp.bfloat16)
        out = dot_nn(delta, gram[TERMS - 1, rows, :])
        for term in range(TERMS - 2, -1, -1):
            out = out + dot_nn(delta, gram[term, rows, :])
        return delta.astype(jnp.float32), out

    chain_arrival(2, 0)
    across_arrival(0, 0)
    across_arrival(0, 1)
    build(0, 1)
    chain_arrival(2, 1)
    build(1, 2)
    chain_arrival(3, 0)
    build(2, 3)
    chain_arrival(3, 1)
    across_arrival(1, 0)
    build(3, 4)
    across_arrival(1, 1)
    build(4, 6)
    across_arrival(2, 0)
    build(6, 8)
    across_arrival(2, 1)
    d0, v0 = deltas(0, 2)
    across_arrival(3, 0)
    across_arrival(3, 1)
    d2, v2 = deltas(2, 3)
    early = v0 + v2
    d3, v3 = deltas(3, 4)
    v = early + v3

    delta_all = jnp.concatenate([d0, d2, d3], axis=1)
    terms = jnp.concatenate(split_terms(delta_all * v, 3), axis=0)
    sums = dot_nn(terms, cpty_cols[...])
    quad = sums[:path_share] + (sums[path_share:2 * path_share] + sums[2 * path_share:])
    margin = jnp.sqrt(quad + 1e-06)
    ratio_terms = jnp.concatenate(split_terms(spread / margin, 3), axis=0)
    spans = dot_nn(ratio_terms, cpty_hot[...])
    ratio = spans[:path_share] + (spans[path_share:2 * path_share] + spans[2 * path_share:])
    bar_buf[...] = (ratio * v).astype(jnp.bfloat16)

    def a_piece(zz, xx, p):
        return adj_ref.at[zz * 2 + xx, :, pl.ds(p * adj_span, adj_span)]

    def a_up(zz, p):
        ref = a_piece(zz, x, p)
        sem = zz * ADJ_PIECES + p
        return send(ref, ref, az_u.at[sem], az_r.at[sem], (z + 1) * 2 + x, k)

    def a_down(zz, p):
        ref = a_piece(zz, x, p)
        sem = zz * ADJ_PIECES + p
        return send(ref, ref, az_d.at[sem], az_r.at[sem], (z - 1) * 2 + x, k)

    def a_across(zz, xx, p):
        ref = a_piece(zz, xx, p)
        sem = zz * ADJ_PIECES + p
        return send(ref, ref, ax_s.at[sem], ax_r.at[sem], z * 2 + 1 - x, k)

    def out_copy(where):
        return pltpu.make_async_copy(adj_ref.at[where], adj_out.at[where], outs.at[where])

    for p in range(ADJ_PIECES):
        if p % (ADJ_PIECES // PIECES) == 0:
            wide = slice(p * adj_span, p * adj_span + span)
            coef_all = held[:, :, wide].reshape(trades, span)
            adj_ref[t, :, wide] = dot_nn(bar_buf[...], coef_all).astype(jnp.bfloat16)

        @pl.when(z < DEEP - 1)
        def _():
            a_up(z, p).start()

        @pl.when(z > 0)
        def _():
            a_down(z, p).start()

        a_across(z, x, p).start()
    out_copy(t).start()

    flipped = jnp.concatenate([margin, margin], axis=0).T[:, :path_share]
    msend[...] = flipped.reshape(owners, cpty_dev, path_share)

    def margin_copy(step):
        to = (t + step) % owners
        return send(msend.at[to], mrecv.at[step], ms.at[step], mr.at[step], to, k)

    for step in range(1, owners):
        margin_copy(step).start()

    for j in range(1, DEEP):
        for p in range(ADJ_PIECES):
            @pl.when(z - j >= 0)
            def _():
                a_up(z - j, p).wait_recv()

                @pl.when(z < DEEP - 1)
                def _():
                    a_up(z - j, p).start()
                a_across(z - j, x, p).start()

            @pl.when(z + j < DEEP)
            def _():
                a_down(z + j, p).wait_recv()

                @pl.when(z > 0)
                def _():
                    a_down(z + j, p).start()
                a_across(z + j, x, p).start()

        @pl.when(z - j >= 0)
        def _():
            out_copy((z - j) * 2 + x).start()

        @pl.when(z + j < DEEP)
        def _():
            out_copy((z + j) * 2 + x).start()

    for step in range(1, owners):
        margin_copy(step).wait_recv()
    mrecv[0] = msend[t]
    for first in range(0, owners, 2):
        pair = [mrecv[(t - o) % owners] for o in (first, first + 1)]
        margin_ref[:, first * path_share:(first + 2) * path_share] = jnp.concatenate(pair, axis=1)
    margin_done = pltpu.make_async_copy(margin_ref, margin_out, local.at[0])
    margin_done.start()

    def adj_across(zz):
        for p in range(ADJ_PIECES):
            a_across(zz, 1 - x, p).wait_recv()
        out_copy(zz * 2 + 1 - x).start()

    adj_across(z)
    for j in range(1, DEEP):
        @pl.when(z - j >= 0)
        def _():
            adj_across(z - j)

        @pl.when(z + j < DEEP)
        def _():
            adj_across(z + j)

    for step in range(1, owners):
        msg_copy(step).wait_send()
        margin_copy(step).wait_send()
    for p in range(PIECES):
        for where in range(owners):
            @pl.when(where != own)
            def _():
                over(where, p).wait_send()
        for zz in range(DEEP):
            across(zz, p).wait_send()

            @pl.when((zz <= z) & (z < DEEP - 1))
            def _():
                up(zz, p).wait_send()

            @pl.when((zz >= z) & (z > 0))
            def _():
                down(zz, p).wait_send()
    for p in range(ADJ_PIECES):
        for zz in range(DEEP):
            a_across(zz, x, p).wait_send()

            @pl.when((zz <= z) & (z < DEEP - 1))
            def _():
                a_up(zz, p).wait_send()

            @pl.when((zz >= z) & (z > 0))
            def _():
                a_down(zz, p).wait_send()
    margin_done.wait()
    for where in range(owners):
        out_copy(where).wait()


def hand_over(adj_in, margin_in, adj_out, margin_out, adj_held, margin_held, sems):
    count = adj_in.shape[0]
    legs = [(adj_in.at[i], adj_held.at[i], adj_out.at[i]) for i in range(count)]
    legs.append((margin_in, margin_held, margin_out))
    reads = [pltpu.make_async_copy(a, b, sems.at[i]) for i, (a, b, _) in enumerate(legs)]
    writes = [
        pltpu.make_async_copy(b, c, sems.at[count + 1 + i]) for i, (_, b, c) in enumerate(legs)
    ]
    for copy in reads:
        copy.start()
    for read, write in zip(reads, writes):
        read.wait()
        write.start()
    for copy in writes:
        copy.wait()


def split_paths(
    basis_values, coefficients, trade_cpty, trade_bucket, risk_weights, correlation, funding_spread
):
    owners = lax.axis_size("trade")
    per_device, width = coefficients.shape
    cpty_dev = funding_spread.shape[0]
    buckets = risk_weights.shape[0]
    path_rows = basis_values.shape[0]
    path_share = path_rows // owners
    trades = owners * per_device
    cptys = owners * cpty_dev
    hbm = pl.BlockSpec(memory_space=pltpu.HBM)
    dma = pltpu.SemaphoreType.DMA
    f32, i32, bf16 = jnp.float32, jnp.int32, jnp.bfloat16
    msg_lanes = -(-per_device // 128) * 128 + 128
    pieces = DEEP * PIECES
    adj_pieces = DEEP * ADJ_PIECES
    adj, margin = pl.pallas_call(
        functools.partial(margin_kernel, owners),
        out_shape=(
            jax.ShapeDtypeStruct((owners, path_share, width), bf16),
            jax.ShapeDtypeStruct((cpty_dev, path_rows), f32),
        ),
        in_specs=[hbm] * 7,
        out_specs=(hbm, hbm),
        scratch_shapes=[
            pltpu.VMEM((owners * 2, per_device // 2, width), bf16),
            pltpu.VMEM((owners, path_share, width), bf16),
            pltpu.VMEM((cpty_dev, path_rows), f32),
            pltpu.VMEM((path_share, width), bf16),
            pltpu.VMEM((1, per_device), i32),
            pltpu.VMEM((1, per_device), i32),
            pltpu.VMEM((1, buckets), f32),
            pltpu.VMEM((buckets, buckets), f32),
            pltpu.VMEM((1, cpty_dev), f32),
            pltpu.VMEM((1, msg_lanes), f32),
            pltpu.VMEM((owners, 1, msg_lanes), f32),
            pltpu.VMEM((TERMS, trades, trades), bf16),
            pltpu.VMEM((trades, 8), i32),
            pltpu.VMEM((buckets, trades), bf16),
            pltpu.VMEM((cptys, trades), bf16),
            pltpu.VMEM((trades, cptys), bf16),
            pltpu.VMEM((path_share, trades), bf16),
            pltpu.VMEM((owners, cpty_dev, path_share), f32),
            pltpu.VMEM((owners, cpty_dev, path_share), f32),
            dma((8,)), dma((pieces,)), dma((pieces,)), dma((pieces,)), dma((pieces,)), dma((pieces,)),
            dma((owners * PIECES,)), dma((owners * PIECES,)),
            dma((owners,)), dma((owners,)), dma((owners,)), dma((owners,)),
            dma((adj_pieces,)), dma((adj_pieces,)), dma((adj_pieces,)), dma((adj_pieces,)),
            dma((adj_pieces,)), dma((owners,)),
        ],
        compiler_params=pltpu.CompilerParams(
            collective_id=0, has_side_effects=True, vmem_limit_bytes=56 * 1024 * 1024
        ),
    )(
        basis_values, coefficients, trade_cpty[None, :], trade_bucket[None, :],
        risk_weights[None, :], correlation, funding_spread[None, :],
    )
    adj, margin = pl.pallas_call(
        hand_over,
        out_shape=(
            jax.ShapeDtypeStruct(adj.shape, bf16), jax.ShapeDtypeStruct(margin.shape, f32),
        ),
        in_specs=[hbm, hbm],
        out_specs=(hbm, hbm),
        scratch_shapes=[
            pltpu.VMEM(adj.shape, bf16), pltpu.VMEM(margin.shape, f32), dma((2 * owners + 2,)),
        ],
        compiler_params=pltpu.CompilerParams(vmem_limit_bytes=56 * 1024 * 1024),
    )(adj, margin)
    return (margin, adj.reshape(path_rows, width))


def margin_terms(arrived, got_codes, risk_weights, correlation, funding_spread):
    path_rows = arrived.shape[0]
    cpty_count = funding_spread.shape[0]
    bucket_count = risk_weights.shape[0]
    is_filled = got_codes >= 0
    column_ids = jnp.arange(cpty_count * bucket_count, dtype=jnp.int32)
    hot_table = (got_codes[:, None] == column_ids[None, :]).astype(jnp.bfloat16)
    bucket_sums = jnp.dot(arrived, hot_table, preferred_element_type=jnp.float32)
    weighted = (
        bucket_sums.reshape(path_rows, cpty_count, bucket_count) * risk_weights[None, None, :]
    )
    rho_w = jnp.einsum("pcb,db->pcd", weighted, correlation, precision=lax.Precision.HIGHEST)
    margin_now = jnp.sqrt(jnp.sum(weighted * rho_w, axis=2) + 1e-06)
    sens_bar = (
        funding_spread[None, :, None] * risk_weights[None, None, :] * rho_w / margin_now[:, :, None]
    )
    flat_bar = sens_bar.reshape(path_rows, cpty_count * bucket_count)
    safe_codes = jnp.where(is_filled, got_codes, 0)
    slot_bar = jnp.take(flat_bar, safe_codes, axis=1) * is_filled[None, :].astype(jnp.float32)
    return (margin_now, slot_bar.astype(jnp.bfloat16))


def body(
    basis_values, coefficients, trade_cpty, trade_bucket, risk_weights, correlation, funding_spread
):
    owners = lax.axis_size("trade")
    per_device = coefficients.shape[0]
    capacity = max(2, 2 * per_device // owners)
    slot_total = owners * capacity
    cpty_count = funding_spread.shape[0]
    bucket_count = risk_weights.shape[0]
    path_rows = basis_values.shape[0]
    owner_of = trade_cpty // cpty_count
    trade_code = trade_cpty % cpty_count * bucket_count + trade_bucket
    position = jnp.arange(per_device, dtype=jnp.int32)
    same_owner = owner_of[:, None] == owner_of[None, :]
    earlier = position[None, :] < position[:, None]
    rank_in = jnp.sum((same_owner & earlier).astype(jnp.int32), axis=1)
    slot_index = owner_of * capacity + rank_in
    codes_out = jnp.full((slot_total,), -1, jnp.int32).at[slot_index].set(trade_code)
    got_codes = lax.all_to_all(codes_out, "trade", split_axis=0, concat_axis=0, tiled=True)
    delta_rows = lax.dot_general(
        basis_values, coefficients, (((1,), (1,)), ((), ())), preferred_element_type=jnp.float32
    ).astype(jnp.bfloat16)
    outgoing = jnp.zeros((path_rows, slot_total), jnp.bfloat16).at[:, slot_index].set(delta_rows)
    arrived = lax.all_to_all(outgoing, "trade", split_axis=1, concat_axis=1, tiled=True)
    margin_now, slot_bar = margin_terms(
        arrived, got_codes, risk_weights, correlation, funding_spread
    )
    returned = lax.all_to_all(slot_bar, "trade", split_axis=1, concat_axis=1, tiled=True)
    delta_bar = returned[:, slot_index]
    partial_adj = jnp.dot(delta_bar, coefficients, preferred_element_type=jnp.float32)
    basis_adjoint = lax.psum(partial_adj, "trade").astype(jnp.bfloat16)
    return (margin_now.T, basis_adjoint)


def solution(mesh):
    placed = (
        P(("date", "path"), None),
        P(("date", "trade"), None),
        P("trade"),
        P("trade"),
        P(),
        P(),
        P("trade"),
    )
    whole = split_paths if mesh.shape["trade"] == 2 * DEEP else body
    return jax.shard_map(
        whole,
        mesh=mesh,
        in_specs=placed,
        out_specs=(P("trade", ("date", "path")), P(("date", "path"), None)),
        check_vma=False,
    )
```

profile of v0, /device:TPU:0, one launch (start us, length us, event | category | flops | bytes accessed | tf_op | source)
XLA Modules:
  0.0 38.2 jit_solution(15256302634440096373)
XLA Ops:
  0.6 35.7 %shard_map.86 = (bf16[8,64,512]{2,1,0:T(8,128)(2,1)}, f32[16,512]{1,0:T(8,128)}) custom-call(bf16[512,512]{1,0:T(8,128)(2,1)} %basis_in.1, bf16[160,512]{1,0:T(8,128)(2,1)} %coef_in.1, s32[1,160]{1,0:T(1,128)} %bitcast.5, s32[1,160]{1,0:T(1,128)} %bitcast.6, f32[1,128]{1,0:T(1,128)} %bitcast.7, f32[128,128]{1,0:T(8,128)} %corr_in.1, f32[1,16]{1,0:T(1,128)} %bitcast.8), custom_call_target="tpu_custom_call" | custom-call | tf_op jit(solution)/shard_map/pallas_call | solution.py:464
  36.3 1.9 %shard_map.87 = (bf16[8,64,512]{2,1,0:T(8,128)(2,1)}, f32[16,512]{1,0:T(8,128)}) custom-call(bf16[8,64,512]{2,1,0:T(8,128)(2,1)} %get-tuple-element.6.adj_in, f32[16,512]{1,0:T(8,128)} %get-tuple-element.7.margin_in), custom_call_target="tpu_custom_call" | custom-call | tf_op jit(solution)/shard_map/pallas_call | solution.py:505
where the time goes:
time: 38.4 us; the launch traced here: 38.2 us
  Pallas kernels  37.5 us (98%)
  between operations  0.64 us (2%)
    pallas_call x1, Pallas kernels, split_paths(): pl.pallas_call(functools.partial(margin_kernel, owners), out_shape=(jax.S...  35.7 us
    pallas_call x1, Pallas kernels, split_paths(): pl.pallas_call(hand_over, out_shape=(jax.ShapeDtypeStruct(adj.shape, bf16...  1.86 us

commit v1 on v0

--- a/solution.py
+++ b/solution.py
@@ -194,7 +194,7 @@
         copy.wait()
     rw_rows = jnp.broadcast_to(rw_buf[...], (buckets, buckets))
     scaled = corr_buf[...] * rw_rows * rw_rows.T
-    scaled_terms = jnp.concatenate(split_terms(scaled, TERMS), axis=1)
+    scaled_terms = jnp.concatenate(split_terms(scaled, 3), axis=1)
 
     chain_arrival(1, 0)
     chain_arrival(1, 1)
@@ -233,14 +233,17 @@
             cpty_cols[rows, :] = (
                 lax.broadcasted_iota(jnp.int32, (per_device, cptys), 1) == code_col // buckets
             ).astype(jnp.float32).astype(jnp.bfloat16)
-            picked = dot_nn(hot, scaled_terms).astype(jnp.bfloat16)
-            stacked = jnp.concatenate(
-                [picked[:, term * buckets:(term + 1) * buckets] for term in range(TERMS)], axis=0
+            spread_out = dot_nn(hot, scaled_terms)
+            picked = spread_out[:, :buckets] + (
+                spread_out[:, buckets:2 * buckets] + spread_out[:, 2 * buckets:]
             )
-            blocks = dot_nn(stacked, bucket_hot[...])
-            for term in range(TERMS):
-                block = blocks[term * per_device:(term + 1) * per_device]
-                gram[term, rows, :] = jnp.where(same, block, 0.0).astype(jnp.bfloat16)
+            for first_lane in range(0, trades, buckets):
+                lanes = slice(first_lane, first_lane + buckets)
+                where = jnp.broadcast_to(bucket_row[:, lanes], (per_device, buckets))
+                block = jnp.take_along_axis(picked, where, axis=1, mode="promise_in_bounds")
+                block = jnp.where(same[:, lanes], block, 0.0)
+                for term, part in enumerate(split_terms(block, TERMS)):
+                    gram[term, rows, lanes] = part
 
     def deltas(first, last):
         for where in range(2 * first, 2 * last):

time: 38.4 us -> 39.1 us (1.018)
  Pallas kernels: 37.5 us -> 38.3 us
    pallas_call x1, Pallas kernels: 35.7 us -> 36.4 us  [split_paths(): pl.pallas_call(functools.partial(margin_kernel, owners), out_shape=(jax.S...]
where the time goes in v1:
time: 39.1 us; the launch traced here: 38.9 us
  Pallas kernels  38.3 us (98%)
  between operations  0.64 us (2%)
    pallas_call x1, Pallas kernels, split_paths(): pl.pallas_call(functools.partial(margin_kernel, owners), out_shape=(jax.S...  36.4 us
    pallas_call x1, Pallas kernels, split_paths(): pl.pallas_call(hand_over, out_shape=(jax.ShapeDtypeStruct(adj.shape, bf16...  1.86 us

profile of v1, /device:TPU:0, one launch (start us, length us, event | category | flops | bytes accessed | tf_op | source)
XLA Modules:
  0.0 38.9 jit_solution(5536875566900925239)
XLA Ops:
  0.6 36.4 %shard_map.86 = (bf16[8,64,512]{2,1,0:T(8,128)(2,1)}, f32[16,512]{1,0:T(8,128)}) custom-call(bf16[512,512]{1,0:T(8,128)(2,1)} %basis_in.1, bf16[160,512]{1,0:T(8,128)(2,1)} %coef_in.1, s32[1,160]{1,0:T(1,128)} %bitcast.5, s32[1,160]{1,0:T(1,128)} %bitcast.6, f32[1,128]{1,0:T(1,128)} %bitcast.7, f32[128,128]{1,0:T(8,128)} %corr_in.1, f32[1,16]{1,0:T(1,128)} %bitcast.8), custom_call_target="tpu_custom_call" | custom-call | tf_op jit(solution)/shard_map/pallas_call | solution.py:467
  37.0 1.9 %shard_map.87 = (bf16[8,64,512]{2,1,0:T(8,128)(2,1)}, f32[16,512]{1,0:T(8,128)}) custom-call(bf16[8,64,512]{2,1,0:T(8,128)(2,1)} %get-tuple-element.6.adj_in, f32[16,512]{1,0:T(8,128)} %get-tuple-element.7.margin_in), custom_call_target="tpu_custom_call" | custom-call | tf_op jit(solution)/shard_map/pallas_call | solution.py:508

commit v2 on v0

--- a/solution.py
+++ b/solution.py
@@ -53,7 +53,7 @@
     code_lanes = -(-per_device // 128) * 128
 
     def slot(zz, xx, rz, rx):
-        return (xx + rx) % 2 * 4 + (zz // 2 + rz // 2) % 2 * 2 + zz % 2
+        return (xx + rx) % 2 * 4 + (zz // 2 + rz // 2) % 2 * 2 + (zz + rz // 2) % 2
 
     def send(src, dst, send_sem, recv_sem, to_trade, to_path):
         return pltpu.make_async_remote_copy(
@@ -202,7 +202,7 @@
         msg_copy(step).wait_recv()
 
     def sender(i):
-        zz = (i // 2 + z // 2) % 2 * 2 + i % 2
+        zz = (i // 2 + z // 2) % 2 * 2 + (i + z // 2) % 2
         return zz * 2 + (i // 4 + x) % 2
 
     codes = jnp.concatenate(
@@ -221,17 +221,19 @@
     ).astype(jnp.float32).astype(jnp.bfloat16)
     cols_buf[...] = jnp.broadcast_to(codes.astype(jnp.float32), (8, trades)).T.astype(jnp.int32)
 
+    block_rows = 2 * per_device
+
     def build(first, last):
         @pl.loop(first, last)
         def _(i):
-            rows = pl.ds(pl.multiple_of(i * per_device, 16), per_device)
+            rows = pl.ds(pl.multiple_of(i * block_rows, 16), block_rows)
             code_col = cols_buf[rows, :1]
             hot = (
-                lax.broadcasted_iota(jnp.int32, (per_device, buckets), 1) == code_col % buckets
+                lax.broadcasted_iota(jnp.int32, (block_rows, buckets), 1) == code_col % buckets
             ).astype(jnp.float32).astype(jnp.bfloat16)
             same = code_col // buckets == cpty_row
             cpty_cols[rows, :] = (
-                lax.broadcasted_iota(jnp.int32, (per_device, cptys), 1) == code_col // buckets
+                lax.broadcasted_iota(jnp.int32, (block_rows, cptys), 1) == code_col // buckets
             ).astype(jnp.float32).astype(jnp.bfloat16)
             picked = dot_nn(hot, scaled_terms).astype(jnp.bfloat16)
             stacked = jnp.concatenate(
@@ -239,11 +241,11 @@
             )
             blocks = dot_nn(stacked, bucket_hot[...])
             for term in range(TERMS):
-                block = blocks[term * per_device:(term + 1) * per_device]
+                block = blocks[term * block_rows:(term + 1) * block_rows]
                 gram[term, rows, :] = jnp.where(same, block, 0.0).astype(jnp.bfloat16)
 
     def deltas(first, last):
-        for where in range(2 * first, 2 * last):
+        for where in range(first, last):
             for p in range(PIECES):
                 if where < 2:
                     @pl.when(where != own)
@@ -251,39 +253,42 @@
                         over(where, p).wait_recv()
                 else:
                     over(where, p).wait_recv()
-        rows = slice(first * 2 * per_device, last * 2 * per_device)
-        coef_rows = held[first * 4:last * 4].reshape((last - first) * 2 * per_device, width)
-        delta = dot_nt(rows_buf[...], coef_rows).astype(jnp.bfloat16)
-        out = dot_nn(delta, gram[TERMS - 1, rows, :])
+        coef_rows = held[first * 2:last * 2].reshape((last - first) * per_device, width)
+        return dot_nt(rows_buf[...], coef_rows)
+
+    def spans_of(delta, first, last):
+        out = dot_nn(delta, gram[TERMS - 1, first:last, :])
         for term in range(TERMS - 2, -1, -1):
-            out = out + dot_nn(delta, gram[term, rows, :])
-        return delta.astype(jnp.float32), out
+            out = out + dot_nn(delta, gram[term, first:last, :])
+        return out
 
     chain_arrival(2, 0)
     across_arrival(0, 0)
     across_arrival(0, 1)
     build(0, 1)
     chain_arrival(2, 1)
+    chain_arrival(3, 0)
     build(1, 2)
-    chain_arrival(3, 0)
-    build(2, 3)
     chain_arrival(3, 1)
     across_arrival(1, 0)
+    across_arrival(1, 1)
+    build(2, 3)
+    across_arrival(2, 0)
     build(3, 4)
-    across_arrival(1, 1)
-    build(4, 6)
-    across_arrival(2, 0)
-    build(6, 8)
     across_arrival(2, 1)
-    d0, v0 = deltas(0, 2)
+    cut, tail = trades * 2 // 5, trades * 4 // 5
+    d0 = deltas(0, 4)
+    v = spans_of(d0[:, :cut].astype(jnp.bfloat16), 0, cut)
+    d1 = deltas(4, 7)
     across_arrival(3, 0)
+    middle = jnp.concatenate([d0[:, cut:], d1], axis=1)
+    v = v + spans_of(middle[:, :tail - cut].astype(jnp.bfloat16), cut, tail)
     across_arrival(3, 1)
-    d2, v2 = deltas(2, 3)
-    early = v0 + v2
-    d3, v3 = deltas(3, 4)
-    v = early + v3
-
-    delta_all = jnp.concatenate([d0, d2, d3], axis=1)
+    d2 = deltas(7, 8)
+    delta_all = jnp.concatenate([d0, d1, d2], axis=1).astype(jnp.bfloat16)
+    v = v + spans_of(delta_all[:, tail:], tail, trades)
+    delta_all = delta_all.astype(jnp.float32)
+
     terms = jnp.concatenate(split_terms(delta_all * v, 3), axis=0)
     sums = dot_nn(terms, cpty_cols[...])
     quad = sums[:path_share] + (sums[path_share:2 * path_share] + sums[2 * path_share:])

time: 38.4 us -> 38.7 us (level)
  no operation moved by 1% of the time
where the time goes in v2:
time: 38.7 us; the launch traced here: 38.5 us
  Pallas kernels  37.8 us (98%)
  between operations  0.64 us (2%)
    pallas_call x1, Pallas kernels, split_paths(): pl.pallas_call(functools.partial(margin_kernel, owners), out_shape=(jax.S...  36 us
    pallas_call x1, Pallas kernels, split_paths(): pl.pallas_call(hand_over, out_shape=(jax.ShapeDtypeStruct(adj.shape, bf16...  1.86 us

profile of v2, /device:TPU:0, one launch (start us, length us, event | category | flops | bytes accessed | tf_op | source)
XLA Modules:
  0.0 38.5 jit_solution(17675821066897182945)
XLA Ops:
  0.6 36.0 %shard_map.86 = (bf16[8,64,512]{2,1,0:T(8,128)(2,1)}, f32[16,512]{1,0:T(8,128)}) custom-call(bf16[512,512]{1,0:T(8,128)(2,1)} %basis_in.1, bf16[160,512]{1,0:T(8,128)(2,1)} %coef_in.1, s32[1,160]{1,0:T(1,128)} %bitcast.5, s32[1,160]{1,0:T(1,128)} %bitcast.6, f32[1,128]{1,0:T(1,128)} %bitcast.7, f32[128,128]{1,0:T(8,128)} %corr_in.1, f32[1,16]{1,0:T(1,128)} %bitcast.8), custom_call_target="tpu_custom_call" | custom-call | tf_op jit(solution)/shard_map/pallas_call | solution.py:469
  36.6 1.9 %shard_map.87 = (bf16[8,64,512]{2,1,0:T(8,128)(2,1)}, f32[16,512]{1,0:T(8,128)}) custom-call(bf16[8,64,512]{2,1,0:T(8,128)(2,1)} %get-tuple-element.6.adj_in, f32[16,512]{1,0:T(8,128)} %get-tuple-element.7.margin_in), custom_call_target="tpu_custom_call" | custom-call | tf_op jit(solution)/shard_map/pallas_call | solution.py:510

commit v3 on v2

--- a/solution.py
+++ b/solution.py
@@ -221,7 +221,7 @@
     ).astype(jnp.float32).astype(jnp.bfloat16)
     cols_buf[...] = jnp.broadcast_to(codes.astype(jnp.float32), (8, trades)).T.astype(jnp.int32)
 
-    block_rows = 2 * per_device
+    block_rows = per_device
 
     def build(first, last):
         @pl.loop(first, last)
@@ -267,14 +267,16 @@
     across_arrival(0, 1)
     build(0, 1)
     chain_arrival(2, 1)
+    build(1, 2)
     chain_arrival(3, 0)
-    build(1, 2)
+    build(2, 3)
     chain_arrival(3, 1)
     across_arrival(1, 0)
+    build(3, 4)
     across_arrival(1, 1)
-    build(2, 3)
+    build(4, 6)
     across_arrival(2, 0)
-    build(3, 4)
+    build(6, 8)
     across_arrival(2, 1)
     cut, tail = trades * 2 // 5, trades * 4 // 5
     d0 = deltas(0, 4)

time: 38.7 us -> 39.4 us (1.018)
  Pallas kernels: 37.8 us -> 38.5 us
    pallas_call x1, Pallas kernels: 36 us -> 36.6 us  [split_paths(): pl.pallas_call(functools.partial(margin_kernel, owners), out_shape=(jax.S...]
where the time goes in v3:
time: 39.4 us; the launch traced here: 39.1 us
  Pallas kernels  38.5 us (98%)
  between operations  0.64 us (2%)
    pallas_call x1, Pallas kernels, split_paths(): pl.pallas_call(functools.partial(margin_kernel, owners), out_shape=(jax.S...  36.6 us
    pallas_call x1, Pallas kernels, split_paths(): pl.pallas_call(hand_over, out_shape=(jax.ShapeDtypeStruct(adj.shape, bf16...  1.86 us

profile of v3, /device:TPU:0, one launch (start us, length us, event | category | flops | bytes accessed | tf_op | source)
XLA Modules:
  0.0 39.1 jit_solution(1348193360236601779)
XLA Ops:
  0.6 36.6 %shard_map.86 = (bf16[8,64,512]{2,1,0:T(8,128)(2,1)}, f32[16,512]{1,0:T(8,128)}) custom-call(bf16[512,512]{1,0:T(8,128)(2,1)} %basis_in.1, bf16[160,512]{1,0:T(8,128)(2,1)} %coef_in.1, s32[1,160]{1,0:T(1,128)} %bitcast.5, s32[1,160]{1,0:T(1,128)} %bitcast.6, f32[1,128]{1,0:T(1,128)} %bitcast.7, f32[128,128]{1,0:T(8,128)} %corr_in.1, f32[1,16]{1,0:T(1,128)} %bitcast.8), custom_call_target="tpu_custom_call" | custom-call | tf_op jit(solution)/shard_map/pallas_call | solution.py:471
  37.3 1.9 %shard_map.87 = (bf16[8,64,512]{2,1,0:T(8,128)(2,1)}, f32[16,512]{1,0:T(8,128)}) custom-call(bf16[8,64,512]{2,1,0:T(8,128)(2,1)} %get-tuple-element.6.adj_in, f32[16,512]{1,0:T(8,128)} %get-tuple-element.7.margin_in), custom_call_target="tpu_custom_call" | custom-call | tf_op jit(solution)/shard_map/pallas_call | solution.py:512
